TPU v7x, 32 devices: a whole 2x2x4 slice. The times are simulated.
32 devices in a mesh: groups: 2 (over y), blk: 4 (over z), layer: 2 (over x), rep: 2 (over core).
Axes of the slice: x: 2, y: 2, z: 4, core: 2. Of those that a mesh axis runs over, the one named last changes fastest.
Arguments:
- train_grads: bfloat16 [2, 8192, 4096], P('layer', ('groups', 'blk')), parts along dimension 1, may hold values from -0.29882812 to 0.29882812
- queries: bfloat16 [2, 2, 512, 4096], P('layer', 'rep', ('groups', 'blk')), parts along dimension 2, may hold values from -0.59765625 to 0.59765625
- bases: bfloat16 [2, 64, 128], P('layer', ('blk', 'rep')), may hold values from -0.75 to 0.75
- eigenvalues: float32 [2, 4096], P('layer', ('blk', 'rep')), may hold values from 0.01 to 10
Outputs:
- scores: float32 [2, 256, 8192], P('rep', 'layer', ('groups', 'blk')), parts along dimension 2
There are 2 independent parts, one for each index of `groups`. A program takes and returns all parts, laid end to end along the dimension named above; an argument that names none is the same for every part. Nothing has to cross between parts.
All inputs are finite; a program needn't handle non-finite values.
Results may differ from a plain program's by a relative error of at most 0.0042.
Values may be sent and summed in bfloat16 or wider, within the bound.
A program may use at most 128 MiB of HBM per device.

v0:
```python
import jax
import jax.numpy as jnp
from jax import lax
from jax.sharding import PartitionSpec as P


def rotate_layers(grads, full_bases):
    layer_count, row_count, flat_width = grads.shape
    factor_size = full_bases.shape[1]
    left_basis = full_bases[:, :, :factor_size]
    right_basis = full_bases[:, :, factor_size:]
    grad_square = grads.reshape(layer_count, row_count, factor_size, factor_size)
    half_turn = jnp.einsum(
        "lrab,lbc->lrac", grad_square, right_basis, preferred_element_type=jnp.float32
    ).astype(jnp.bfloat16)
    full_turn = jnp.einsum(
        "lca,lrcb->lrab", left_basis, half_turn, preferred_element_type=jnp.float32
    )
    return full_turn.reshape(layer_count, row_count, flat_width)


def body(train_grads, queries, bases, eigenvalues):
    full_bases = lax.all_gather(bases, ("blk", "rep"), axis=1, tiled=True)
    eigen_full = lax.all_gather(eigenvalues, ("blk", "rep"), axis=1, tiled=True)
    inverse_damped = 1.0 / (eigen_full + 0.1 * jnp.mean(eigen_full, axis=1, keepdims=True))
    train_turned = rotate_layers(train_grads, full_bases).astype(jnp.bfloat16)
    own_queries = queries[:, 0]
    ready = (
        rotate_layers(lax.all_gather(own_queries, "blk", axis=1, tiled=True), full_bases)
        * inverse_damped[:, None, :]
    ).astype(jnp.bfloat16)
    partial_scores = jnp.einsum(
        "lqp,ltp->qt", ready, train_turned, preferred_element_type=jnp.float32
    )
    owned = lax.psum_scatter(partial_scores, "layer", scatter_dimension=0, tiled=True)
    return owned[None]


def solution(mesh):
    return jax.shard_map(
        body,
        mesh=mesh,
        in_specs=(
            P("layer", ("groups", "blk"), None),
            P("layer", "rep", ("groups", "blk"), None),
            P("layer", ("blk", "rep"), None),
            P("layer", ("blk", "rep")),
        ),
        out_specs=P("rep", "layer", ("groups", "blk")),
        check_vma=False,
    )
```

profile of v0, /device:TPU:0, one launch (start us, length us, event | category | flops | bytes accessed | tf_op | source)
XLA Modules:
  0.0 108.9 jit_solution(12992789181235766646)
XLA Ops:
  6.5 0.0 all-gather.3.cloned.1.call-start
  6.5 0.7 all-gather.3.cloned.1.call-update
  7.3 0.0 copy-start
  7.3 0.0 copy-start.1
  7.3 0.0 reduce-scatter.2.cloned.1.call-start
  7.3 12.0 %copy.20 = bf16[1,1024,4096]{1,2,0:T(8,128)(2,1)} copy(bf16[1,1024,4096]{2,1,0:T(8,128)(2,1)} %param.4) | data formatting | bytes 16777216 | tf_op args[0]
  19.3 0.0 copy-done
  19.3 14.6 %all_gather.11 = f32[1,4096]{1,0:T(1,128)S(1)} all-gather(f32[1,512]{1,0:T(1,128)S(1)} %copy-done), channel_id=1, replica_groups=mesh['groups'=2,'blk'=4,'layer'=2,'rep'=2] {'blk','rep'}, dimensions={1}, use_global_device_ids=true | all-gather | bytes 18432 | tf_op jit(solution)/shard_map/all_gather | solution.py:24
  33.9 0.6 reduce_sum.9
  35.3 0.1 mul.19
  35.3 0.1 copy.19
  35.4 0.0 copy-done.1
  35.4 12.8 %all_gather.10 = bf16[1,64,128]{2,1,0:T(8,128)(2,1)S(1)} all-gather(bf16[1,8,128]{2,1,0:T(8,128)(2,1)S(1)} %copy-done.1), channel_id=1, replica_groups=mesh['groups'=2,'blk'=4,'layer'=2,'rep'=2] {'blk','rep'}, dimensions={1}, use_global_device_ids=true | all-gather | bytes 18432 | tf_op jit(solution)/shard_map/all_gather | solution.py:23
  48.2 9.1 %convolution_convert_fusion = bf16[1024,64,64]{0,2,1:T(8,128)(2,1)} fusion(bf16[1024,64,64]{0,2,1:T(8,128)(2,1)} %bitcast.42, bf16[1,64,128]{2,1,0:T(8,128)(2,1)S(1)} %all_gather.10), kind=kOutput, calls=%fused_computation.5 | convolution fusion | flops 541065216 | bytes 16793600 | tf_op jit(solution)/shard_map/lrab,lbc->lrac/dot_general | solution.py:13
  57.2 0.7 all-gather.3.cloned.1.call-done
  57.9 3.3 %copy.15 = bf16[1,1,256,4096]{2,3,1,0:T(8,128)(2,1)S(1)} copy(bf16[1,1,256,4096]{3,2,1,0:T(8,128)(2,1)} %all-gather.3.cloned.1.call-done) | data formatting | bytes 4194304 | tf_op jit(solution)/shard_map/all_gather | solution.py:29
  61.2 0.8 convolution_convert_fusion.1
  62.0 3.4 %fusion.9 = bf16[1,256,64,64]{1,2,3,0:T(8,128)(2,1)S(1)} fusion(bf16[256,64,64]{0,2,1:T(8,128)(2,1)S(1)} %convolution_convert_fusion.1, f32[64,64]{0,1:T(8,128)S(1)} %copy.19, bf16[1,64,128]{2,1,0:T(8,128)(2,1)S(1)} %all_gather.10), kind=kOutput, calls=%fused_computation.7 | convolution fusion | flops 136314880 | bytes 4227072 | tf_op jit(solution)/shard_map/lca,lrcb->lrab/dot_general | solution.py:16
  65.4 17.5 %fusion.12 = f32[256,1024]{1,0:T(8,128)} fusion(bf16[1024,64,64]{0,2,1:T(8,128)(2,1)} %convolution_convert_fusion, bf16[1,256,64,64]{1,2,3,0:T(8,128)(2,1)S(1)} %fusion.9, bf16[1,64,128]{2,1,0:T(8,128)(2,1)S(1)} %all_gather.10), kind=kOutput, calls=%fused_computation.11 | convolution fusion | flops 2688548864 | bytes 11550720 | tf_op jit(solution)/shard_map/lqp,ltp->qt/dot_general | solution.py:32
  82.9 0.0 reduce-scatter.2.cloned.1.call-update
  82.9 19.2 %reduce-scatter.2.cloned.1.call-done = f32[128,1024]{1,0:T(8,128)} async-done(((f32[256,1024]{1,0:T(8,128)}), f32[128,1024]{1,0:T(8,128)}) %reduce-scatter.2.cloned.1.call-update) | async-done | bytes 524304 | tf_op jit(solution)/shard_map/reduce_scatter | solution.py:35
  (1 shorter events, 0.0 us)
Async XLA Ops:
  6.5 51.4 %all-gather.3.cloned.1.call-start = ((), (), s32[]{:S(2)}) async-start(), calls=%async_computation.2 | async-start | bytes 2621440 | tf_op jit(solution)/shard_map/all_gather | solution.py:29
  7.3 12.0 %copy-start = (f32[1,512]{1,0:T(1,128)S(1)}, f32[1,512]{1,0:T(1,128)}, u32[]{:S(2)}) copy-start(f32[1,512]{1,0:T(1,128)} %param.7) | copy-start | bytes 6148
  7.3 28.1 %copy-start.1 = (bf16[1,8,128]{2,1,0:T(8,128)(2,1)S(1)}, bf16[1,8,128]{2,1,0:T(8,128)(2,1)}, u32[]{:S(2)}) copy-start(bf16[1,8,128]{2,1,0:T(8,128)(2,1)} %param.6) | copy-start | bytes 6148
  7.3 94.8 %reduce-scatter.2.cloned.1.call-start = ((), (), s32[]{:S(2)}) async-start(), calls=%async_computation.1 | async-start | bytes 1572864 | tf_op jit(solution)/shard_map/reduce_scatter | solution.py:35
Sparse Core Ops, SparseCore 0:
  8.9 48.9 all-gather.2
  83.0 18.9 reduce-scatter.1
where the time goes:
time: 109 us
  matrix products  30.7 us (28%)
  blocking collectives  27.4 us (25%)
  waiting for transfers between devices  20.6 us (19%)
  local copies, waits for them, and re-layouts  15.4 us (14%)
  between operations  14.1 us (13%)
    reduce_scatter x1, waiting for transfers between devices, body(): lax.psum_scatter(partial_scores, 'layer', scatter_dimension=0, tiled=True)  19.2 us
    dot_general x1, matrix products, body(): jnp.einsum('lqp,ltp->qt', ready, train_turned, preferred_element_type=jnp...  17.5 us
    all_gather x1, blocking collectives, body(): eigen_full = lax.all_gather(eigenvalues, ('blk', 'rep'), axis=1, tiled=True)  14.6 us
    all_gather x1, blocking collectives, body(): full_bases = lax.all_gather(bases, ('blk', 'rep'), axis=1, tiled=True)  12.8 us
    unnamed x5, local copies, waits for them, and re-layouts  12 us
    dot_general x2, matrix products, rotate_layers(): jnp.einsum('lrab,lbc->lrac', grad_square, right_basis, preferred_element_...  9.85 us
    dot_general x1, matrix products, rotate_layers(): jnp.einsum('lca,lrcb->lrab', left_basis, half_turn, preferred_element_typ...  3.36 us
    all_gather x1, local copies, waits for them, and re-layouts, body(): lax.all_gather(own_queries, 'blk', axis=1, tiled=True)  3.27 us
  transfers between devices with their start and end apart: 2, of which 2 were waited for; matrix products, arithmetic and copies ran while one was open for 20% of the time, Pallas kernels for 0%

commit v1 on v0

v1 whole, which is shorter than its diff:
```python
import jax
import jax.numpy as jnp
from jax import lax
from jax.sharding import PartitionSpec as P


def spread_queries(queries, full_bases, inverse_damped):
    layer_count, row_count, flat_width = queries.shape
    k = full_bases.shape[1]
    u = full_bases[:, :, :k]
    v = full_bases[:, :, k:]
    square = queries.reshape(layer_count, row_count, k, k)
    f32 = jnp.float32
    half = jnp.einsum("lrab,lbc->lrac", square, v, preferred_element_type=f32).astype(jnp.bfloat16)
    full = jnp.einsum("lca,lrcb->lrab", u, half, preferred_element_type=f32)
    scaled = (full * inverse_damped.reshape(layer_count, 1, k, k)).astype(jnp.bfloat16)
    back = jnp.einsum("lca,lrab->lrcb", u, scaled, preferred_element_type=f32).astype(jnp.bfloat16)
    out = jnp.einsum("lrac,lbc->lrab", back, v, preferred_element_type=f32).astype(jnp.bfloat16)
    return out.reshape(layer_count, row_count, flat_width)


def body(train_grads, queries, bases, eigenvalues):
    full_bases = lax.all_gather(bases, ("blk", "rep"), axis=1, tiled=True)
    eigen_full = lax.all_gather(eigenvalues, ("blk", "rep"), axis=1, tiled=True)
    inverse_damped = 1.0 / (eigen_full + 0.1 * jnp.mean(eigen_full, axis=1, keepdims=True))
    ready = spread_queries(queries[:, 0], full_bases, inverse_damped)
    ready = lax.all_gather(ready, "blk", axis=1, tiled=True)
    partial_scores = jnp.einsum(
        "lqp,ltp->qt", ready, train_grads, preferred_element_type=jnp.float32
    )
    owned = lax.psum_scatter(partial_scores, "layer", scatter_dimension=0, tiled=True)
    return owned[None]


def solution(mesh):
    return jax.shard_map(
        body,
        mesh=mesh,
        in_specs=(
            P("layer", ("groups", "blk"), None),
            P("layer", "rep", ("groups", "blk"), None),
            P("layer", ("blk", "rep"), None),
            P("layer", ("blk", "rep")),
        ),
        out_specs=P("rep", "layer", ("groups", "blk")),
        check_vma=False,
    )
```

time: 109 us -> 120 us (1.10)
  waiting for transfers between devices: 20.6 us -> 63.8 us
  matrix products: 30.7 us -> 9.7 us
  local copies, waits for them, and re-layouts: 15.4 us -> 3.82 us
    all_gather x1, waiting for transfers between devices: 0.67 us -> 44.6 us  [body(): ready = lax.all_gather(ready, 'blk', axis=1, tiled=True)]
    dot_general x4 -> x3, matrix products: 30.7 us -> 9.7 us  [the longest x1 7.36 us: body(): jnp.einsum('lqp,ltp->qt', ready, train_grads, preferred_element_type=jnp....]
    unnamed x5 -> x0, local copies, waits for them, and re-layouts: 12 us -> none
    reshape x0 -> x2, local copies, waits for them, and re-layouts: none -> 3.67 us
    all_gather x1 -> x0, local copies, waits for them, and re-layouts: 3.27 us -> none  [body(): lax.all_gather(own_queries, 'blk', axis=1, tiled=True)]
    all_gather x1, blocking collectives: 14.6 us -> 12.8 us  [body(): eigen_full = lax.all_gather(eigenvalues, ('blk', 'rep'), axis=1, tiled=True)]
    all_gather x1, blocking collectives: 12.8 us -> 14.5 us  [body(): full_bases = lax.all_gather(bases, ('blk', 'rep'), axis=1, tiled=True)]
  transfers between devices with their start and end apart: 2 -> 2, of which waited for: 2 -> 2; matrix products, arithmetic and copies ran while one was open for 20% -> 0% of each run, Pallas kernels for 0% -> 0%
where the time goes in v1:
time: 120 us
  waiting for transfers between devices  63.8 us (53%)
  blocking collectives  27.3 us (23%)
  between operations  14.1 us (12%)
  matrix products  9.7 us (8%)
  local copies, waits for them, and re-layouts  3.82 us (3%)
    all_gather x1, waiting for transfers between devices, body(): ready = lax.all_gather(ready, 'blk', axis=1, tiled=True)  44.6 us
    reduce_scatter x1, waiting for transfers between devices, body(): lax.psum_scatter(partial_scores, 'layer', scatter_dimension=0, tiled=True)  19.2 us
    all_gather x1, blocking collectives, body(): full_bases = lax.all_gather(bases, ('blk', 'rep'), axis=1, tiled=True)  14.5 us
    all_gather x1, blocking collectives, body(): eigen_full = lax.all_gather(eigenvalues, ('blk', 'rep'), axis=1, tiled=True)  12.8 us
    dot_general x1, matrix products, body(): jnp.einsum('lqp,ltp->qt', ready, train_grads, preferred_element_type=jnp....  7.36 us
  transfers between devices with their start and end apart: 2, of which 2 were waited for; matrix products, arithmetic and copies ran while one was open for 0% of the time, Pallas kernels for 0%

profile of v1, /device:TPU:0, one launch (start us, length us, event | category | flops | bytes accessed | tf_op | source)
XLA Modules:
  0.0 119.5 jit_solution(17203388712670779257)
XLA Ops:
  6.5 0.0 all-gather.2.cloned.1.call-start
  6.5 14.5 %all_gather.9 = bf16[1,64,128]{2,1,0:T(8,128)(2,1)S(1)} all-gather(bf16[1,8,128]{2,1,0:T(8,128)(2,1)} %param.6), channel_id=1, replica_groups=mesh['groups'=2,'blk'=4,'layer'=2,'rep'=2] {'blk','rep'}, dimensions={1}, use_global_device_ids=true | all-gather | bytes 18432 | tf_op jit(solution)/shard_map/all_gather | solution.py:23
  21.0 12.8 %all_gather.10 = f32[1,4096]{1,0:T(1,128)S(1)} all-gather(f32[1,512]{1,0:T(1,128)} %param.7), channel_id=1, replica_groups=mesh['groups'=2,'blk'=4,'layer'=2,'rep'=2] {'blk','rep'}, dimensions={1}, use_global_device_ids=true | all-gather | bytes 18432 | tf_op jit(solution)/shard_map/all_gather | solution.py:24
  33.9 0.6 reduce_sum.9
  35.2 0.1 mul.15
  35.3 0.1 copy.5
  35.4 2.1 %reshape.48 = bf16[64,64,64]{2,1,0:T(8,128)(2,1)S(1)} reshape(bf16[1,1,64,4096]{3,2,1,0:T(8,128)(2,1)} %param.5) | data formatting | bytes 1048576 | tf_op jit(solution)/shard_map/reshape
  37.4 1.5 %fusion.5 = bf16[64,64,64]{1,2,0:T(8,128)(2,1)S(1)} fusion(bf16[64,64,64]{2,1,0:T(8,128)(2,1)S(1)} %reshape.48, f32[64,64]{0,1:T(8,128)S(1)} %copy.5, bf16[1,64,128]{2,1,0:T(8,128)(2,1)S(1)} %all_gather.9), kind=kOutput, calls=%fused_computation.9 | convolution fusion | flops 67895296 | bytes 1638400 | tf_op jit(solution)/shard_map/lca,lrcb->lrab/dot_general | solution.py:15
  38.9 0.8 convolution_convert_fusion
  39.8 1.6 %reshape.53 = bf16[1,64,4096]{2,1,0:T(8,128)(2,1)} reshape(bf16[64,64,64]{2,1,0:T(8,128)(2,1)S(1)} %convolution_convert_fusion) | data formatting | bytes 1048576 | tf_op jit(solution)/shard_map/reshape | solution.py:19
  41.4 0.0 all-gather.2.cloned.1.call-update
  41.4 0.0 reduce-scatter.2.cloned.1.call-start
  41.5 44.6 %all-gather.2.cloned.1.call-done = bf16[1,256,4096]{2,1,0:T(8,128)(2,1)} async-done(((bf16[1,64,4096]{2,1,0:T(8,128)(2,1)}), bf16[1,256,4096]{2,1,0:T(8,128)(2,1)}) %all-gather.2.cloned.1.call-update) | async-done | bytes 2097168 | tf_op jit(solution)/shard_map/all_gather | solution.py:27
  86.1 7.4 %fusion = f32[256,1024]{1,0:T(8,128)} fusion(bf16[1,1024,4096]{2,1,0:T(8,128)(2,1)} %param.4, bf16[1,256,4096]{2,1,0:T(8,128)(2,1)} %all-gather.2.cloned.1.call-done), kind=kOutput, calls=%fused_computation | convolution fusion | flops 2147483648 | bytes 11534336 | tf_op jit(solution)/shard_map/lqp,ltp->qt/dot_general | solution.py:28
  93.5 0.0 reduce-scatter.2.cloned.1.call-update
  93.5 19.2 %reduce-scatter.2.cloned.1.call-done = f32[128,1024]{1,0:T(8,128)} async-done(((f32[256,1024]{1,0:T(8,128)}), f32[128,1024]{1,0:T(8,128)}) %reduce-scatter.2.cloned.1.call-update) | async-done | bytes 524304 | tf_op jit(solution)/shard_map/reduce_scatter | solution.py:31
  (1 shorter events, 0.0 us)
Async XLA Ops:
  6.5 79.6 %all-gather.2.cloned.1.call-start = ((), (), s32[]{:S(2)}) async-start(), calls=%async_computation.1 | async-start | bytes 2621440 | tf_op jit(solution)/shard_map/all_gather | solution.py:27
  41.4 71.2 %reduce-scatter.2.cloned.1.call-start = ((), (), s32[]{:S(2)}) async-start(), calls=%async_computation.2 | async-start | bytes 1572864 | tf_op jit(solution)/shard_map/reduce_scatter | solution.py:31
Sparse Core Ops, SparseCore 0:
  41.6 44.4 all-gather.1
  93.6 19.0 reduce-scatter.1

commit v2 on v1

v2 whole, which is shorter than its diff:
```python
import functools
import jax
import jax.numpy as jnp
from jax import lax
from jax.experimental import pallas as pl
from jax.experimental.pallas import tpu as pltpu
from jax.sharding import PartitionSpec as P

MESH = pl.DeviceIdType.MESH
F32 = jnp.float32
BF16 = jnp.bfloat16
LANES = 128
CHUNKS = 4


def mm(a, b):
    return jnp.dot(a, b, preferred_element_type=F32)


def mm_t(a, b):
    return lax.dot_general(a, b, (((1,), (1,)), ((), ())), preferred_element_type=F32)


def one_hot(cond):
    return jnp.where(cond, 1.0, 0.0).astype(BF16)


def iota(shape, dim):
    return lax.broadcasted_iota(jnp.int32, shape, dim)


def kernel(
    n_blk, n_rep, n_layer,
    train_hbm, query_hbm, bases_ref, eigen_ref, out_ref,
    train, query, packet, packets, basis, eigen, square, gathered, total, sent, got,
    train_sem, query_sem, pack_send, pack_recv,
    up_send, up_recv, down_send, down_recv, ex_send, ex_recv,
):
    z = lax.axis_index("blk")
    rep = lax.axis_index("rep")
    layer = lax.axis_index("layer")
    n_peer = n_blk * n_rep
    me = z * n_rep + rep
    basis_rows = bases_ref.shape[1]
    eigen_rows = eigen_ref.shape[1] // LANES
    rows, flat = query.shape
    k = basis.shape[0]
    cols = flat // CHUNKS
    seqs = train.shape[1]
    share = n_blk // n_layer
    pairs = flat // LANES
    width = 2 * LANES

    query_copy = pltpu.make_async_copy(query_hbm.at[0, 0], query, query_sem)
    query_copy.start()
    train_copies = [
        pltpu.make_async_copy(
            train_hbm.at[0, :, pl.ds(c * cols, cols)], train.at[c], train_sem.at[c]
        )
        for c in range(CHUNKS)
    ]
    for copy in train_copies:
        copy.start()

    barrier = pltpu.get_barrier_semaphore()
    peers = []
    for d in range(1, n_peer):
        peer = lax.rem(me + d, n_peer)
        peers.append({"blk": peer // n_rep, "rep": lax.rem(peer, n_rep)})
    for peer in peers:
        pl.semaphore_signal(barrier, inc=1, device_id=peer, device_id_type=MESH)
    for d in range(1, n_layer):
        pl.semaphore_signal(
            barrier, inc=1, device_id={"layer": lax.rem(layer + d, n_layer)}, device_id_type=MESH
        )

    packet[...] = jnp.zeros_like(packet)
    packet[0:basis_rows, :] = bases_ref[0].astype(F32)
    for j in range(eigen_rows):
        packet[basis_rows + j:basis_rows + j + 1, :] = eigen_ref[:, j * LANES:(j + 1) * LANES]
    pl.semaphore_wait(barrier, n_peer - 1 + n_layer - 1)

    pack_copies = []
    for d in range(1, n_peer):
        copy = pltpu.make_async_remote_copy(
            src_ref=packet, dst_ref=packets.at[me],
            send_sem=pack_send.at[d], recv_sem=pack_recv.at[d],
            device_id=peers[d - 1], device_id_type=MESH,
        )
        copy.start()
        pack_copies.append(copy)
    packets[me] = packet[...]
    total[...] = jnp.zeros_like(total)

    wide_row, wide_col = iota((width, width), 0), iota((width, width), 1)
    row_k, col_k = iota((width, k), 0), iota((width, k), 1)
    pick_u = one_hot(col_k == 2 * (row_k & (pairs - 1)) + row_k // LANES)
    pick_v = one_hot(col_k == (row_k & (k - 1)))
    same_u = (wide_row & (LANES - 1)) // pairs == (wide_col & (LANES - 1)) // pairs
    same_v = wide_row // k == wide_col // k

    for copy in pack_copies:
        copy.wait_recv()
    for i in range(n_peer):
        basis[i * basis_rows:(i + 1) * basis_rows, :] = packets[i, 0:basis_rows, :]
        eigen[i * eigen_rows:(i + 1) * eigen_rows, :] = packets[
            i, basis_rows:basis_rows + eigen_rows, :
        ]

    u = basis[:, 0:k].astype(BF16)
    v = basis[:, k:2 * k].astype(BF16)

    def spread(pick, left, same):
        return jnp.where(same, mm_t(left, pick), 0.0).astype(BF16)

    u_turn = spread(pick_u, mm(pick_u, u).astype(BF16), same_u)
    u_back = spread(pick_u, mm_t(pick_u, u).astype(BF16), same_u)
    v_turn = spread(pick_v, mm(pick_v, v).astype(BF16), same_v)
    v_back = spread(pick_v, mm_t(pick_v, v).astype(BF16), same_v)

    eig = eigen[...]
    inverse = 1.0 / (eig + 0.1 * (jnp.sum(eig) / flat))
    group = LANES // pairs
    inverse_t = jnp.concatenate([inverse] * group, axis=0).T
    inverse_t = jnp.concatenate([inverse_t[0:k], inverse_t[k:2 * k]], axis=1)
    batch = 4
    inverse_t = jnp.concatenate([inverse_t] * batch, axis=0)

    query_copy.wait()
    for c in range(flat // width):
        half = mm(query[:, c * width:(c + 1) * width], v_turn).astype(BF16).astype(F32)
        for j in range(2):
            square[pl.ds(2 * c + j, rows, stride=pairs), :] = half[:, j * LANES:(j + 1) * LANES]
    for b in range(rows // group // batch):
        stack = []
        for g in range(batch):
            at = (b * batch + g) * LANES
            t = square[at:at + LANES, :].T
            stack.append(jnp.concatenate([t[0:k], t[k:2 * k]], axis=1))
        a = jnp.concatenate(stack, axis=0).astype(BF16)
        scaled = (mm(a, u_turn) * inverse_t).astype(BF16)
        back = mm(scaled, u_back)
        for g in range(batch):
            at = (b * batch + g) * LANES
            part = back[g * k:(g + 1) * k]
            square[at:at + LANES, :] = jnp.concatenate(
                [part[:, 0:LANES], part[:, LANES:width]], axis=0
            ).T

    def up_copy(s, c):
        return pltpu.make_async_remote_copy(
            src_ref=gathered.at[s, c], dst_ref=gathered.at[s, c],
            send_sem=up_send.at[s, c], recv_sem=up_recv.at[s, c],
            device_id={"blk": lax.rem(z + 1, n_blk)}, device_id_type=MESH,
        )

    def down_copy(s, c):
        return pltpu.make_async_remote_copy(
            src_ref=gathered.at[s, c], dst_ref=gathered.at[s, c],
            send_sem=down_send.at[s, c], recv_sem=down_recv.at[s, c],
            device_id={"blk": lax.rem(z + n_blk - 1, n_blk)}, device_id_type=MESH,
        )

    per_chunk = cols // width
    for c in range(flat // width):
        x = jnp.concatenate(
            [square[pl.ds(2 * c + j, rows, stride=pairs), :] for j in range(2)], axis=1
        ).astype(BF16)
        at = (c % per_chunk) * width
        gathered[z, c // per_chunk, :, at:at + width] = mm(x, v_back).astype(BF16)
        if c % per_chunk == per_chunk - 1:
            done = c // per_chunk

            @pl.when(z > 0)
            def _():
                down_copy(z, done).start()

            @pl.when(z < n_blk - 1)
            def _():
                up_copy(z, done).start()

    def score(s, c):
        x = gathered[s, c]
        tile = 256

        def one(t, carry):
            at = pl.ds(pl.multiple_of(t * tile, tile), tile)
            total[s, :, at] += mm_t(x, train[c, at, :])
            return carry

        lax.fori_loop(0, seqs // tile, one, 0)

    def ex_copy(s):
        owner = s // share
        return pltpu.make_async_remote_copy(
            src_ref=sent.at[s], dst_ref=got.at[layer, lax.rem(s, share)],
            send_sem=ex_send.at[s], recv_sem=ex_recv.at[layer, lax.rem(s, share)],
            device_id={"layer": owner}, device_id_type=MESH,
        )

    def finish(s):
        @pl.when(s // share != layer)
        def _():
            sent[s] = total[s].astype(BF16)
            ex_copy(s).start()

    for copy in train_copies:
        copy.wait()

    def own(c, carry):
        score(z, c)
        return carry

    lax.fori_loop(0, CHUNKS, own, 0)
    finish(z)

    def step(i, carry):
        far = 1 + i // CHUNKS
        c = lax.rem(i, CHUNKS)
        above, below = z + far, z - far

        @pl.when(above < n_blk)
        def _():
            down_copy(above, c).wait_recv()

            @pl.when(z > 0)
            def _():
                down_copy(above, c).start()

        @pl.when(below >= 0)
        def _():
            up_copy(below, c).wait_recv()

            @pl.when(z < n_blk - 1)
            def _():
                up_copy(below, c).start()

        @pl.when(above < n_blk)
        def _():
            score(above, c)

            @pl.when(c == CHUNKS - 1)
            def _():
                finish(above)

        @pl.when(below >= 0)
        def _():
            score(below, c)

            @pl.when(c == CHUNKS - 1)
            def _():
                finish(below)

        return carry

    lax.fori_loop(0, (n_blk - 1) * CHUNKS, step, 0)

    for at in range(share):
        mine = layer * share + at
        for other in range(n_layer):
            @pl.when(layer != other)
            def _():
                pltpu.make_async_remote_copy(
                    src_ref=sent.at[0], dst_ref=got.at[other, at],
                    send_sem=ex_send.at[0], recv_sem=ex_recv.at[other, at],
                    device_id={"layer": other}, device_id_type=MESH,
                ).wait_recv()
                total[mine] += got[other, at].astype(F32)
        out_ref[at * rows:(at + 1) * rows, :] = total[mine]

    for copy in pack_copies:
        copy.wait_send()

    def drain(i, carry):
        s, c = i // CHUNKS, lax.rem(i, CHUNKS)

        @pl.when((s >= z) & (z > 0))
        def _():
            down_copy(s, c).wait_send()

        @pl.when((s <= z) & (z < n_blk - 1))
        def _():
            up_copy(s, c).wait_send()

        @pl.when((c == 0) & (s // share != layer))
        def _():
            ex_copy(s).wait_send()

        return carry

    lax.fori_loop(0, n_blk * CHUNKS, drain, 0)


def body(n_blk, n_rep, n_layer, train_grads, queries, bases, eigenvalues):
    seqs, flat = train_grads.shape[1:]
    rows = queries.shape[2]
    k = bases.shape[2] // 2
    n_peer = n_blk * n_rep
    packet_rows = -(-(bases.shape[1] + eigenvalues.shape[1] // LANES) // 8) * 8
    share = n_blk // n_layer
    cols = flat // CHUNKS
    vmem = pl.BlockSpec(memory_space=pltpu.VMEM)
    hbm = pl.BlockSpec(memory_space=pl.ANY)
    dma = pltpu.SemaphoreType.DMA
    out = pl.pallas_call(
        functools.partial(kernel, n_blk, n_rep, n_layer),
        out_shape=jax.ShapeDtypeStruct((share * rows, seqs), F32),
        in_specs=[hbm, hbm, vmem, vmem],
        out_specs=vmem,
        scratch_shapes=[
            pltpu.VMEM((CHUNKS, seqs, cols), BF16),
            pltpu.VMEM((rows, flat), BF16),
            pltpu.VMEM((packet_rows, LANES), F32),
            pltpu.VMEM((n_peer, packet_rows, LANES), F32),
            pltpu.VMEM((k, 2 * k), F32),
            pltpu.VMEM((flat // LANES, LANES), F32),
            pltpu.VMEM((rows * flat // LANES, LANES), F32),
            pltpu.VMEM((n_blk, CHUNKS, rows, cols), BF16),
            pltpu.VMEM((n_blk, rows, seqs), F32),
            pltpu.VMEM((n_blk, rows, seqs), BF16),
            pltpu.VMEM((n_layer, share, rows, seqs), BF16),
            dma((CHUNKS,)),
            dma,
            dma((n_peer,)),
            dma((n_peer,)),
            dma((n_blk, CHUNKS)),
            dma((n_blk, CHUNKS)),
            dma((n_blk, CHUNKS)),
            dma((n_blk, CHUNKS)),
            dma((n_blk,)),
            dma((n_layer, share)),
        ],
        compiler_params=pltpu.CompilerParams(
            collective_id=0, has_side_effects=True, vmem_limit_bytes=52 * 2**20
        ),
        name="influence",
    )(train_grads, queries, bases, eigenvalues)
    return out[None]


def solution(mesh):
    sizes = mesh.shape
    return jax.shard_map(
        functools.partial(body, sizes["blk"], sizes["rep"], sizes["layer"]),
        mesh=mesh,
        in_specs=(
            P("layer", ("groups", "blk"), None),
            P("layer", "rep", ("groups", "blk"), None),
            P("layer", ("blk", "rep"), None),
            P("layer", ("blk", "rep")),
        ),
        out_specs=P("rep", "layer", ("groups", "blk")),
        check_vma=False,
    )
```

time: 120 us -> 54.5 us (0.45)
  waiting for transfers between devices: 63.8 us -> 0 us
  Pallas kernels: 0 us -> 51.1 us
  blocking collectives: 27.3 us -> 0 us
  between operations: 14.1 us -> 0.01 us
  matrix products: 9.7 us -> 0 us
    pallas_call x0 -> x1, Pallas kernels: none -> 51.1 us  [body(): pl.pallas_call(functools.partial(kernel, n_blk, n_rep, n_layer), out_shap...]
    all_gather x1 -> x0, waiting for transfers between devices: 44.6 us -> none  [body(): ready = lax.all_gather(ready, 'blk', axis=1, tiled=True)]
    all_gather x2 -> x0, blocking collectives: 27.3 us -> none  [the longest x1 14.5 us: body(): full_bases = lax.all_gather(bases, ('blk', 'rep'), axis=1, tiled=True)]
    reduce_scatter x1 -> x0, waiting for transfers between devices: 19.2 us -> none  [body(): lax.psum_scatter(partial_scores, 'layer', scatter_dimension=0, tiled=True)]
    dot_general x3 -> x0, matrix products: 9.7 us -> none  [the longest x1 7.36 us: body(): jnp.einsum('lqp,ltp->qt', ready, train_grads, preferred_element_type=jnp....]
    reshape x2 -> x0, local copies, waits for them, and re-layouts: 3.67 us -> none
    unnamed x0 -> x7, local copies, waits for them, and re-layouts: none -> 3.2 us
  transfers between devices with their start and end apart: 2 -> 0, of which waited for: 2 -> 0; matrix products, arithmetic and copies ran while one was open for 0% -> 0% of each run, Pallas kernels for 0% -> 0%
where the time goes in v2:
time: 54.5 us; the launch traced here: 54.3 us
  Pallas kernels  51.1 us (94%)
  local copies, waits for them, and re-layouts  3.2 us (6%)
    pallas_call x1, Pallas kernels, body(): pl.pallas_call(functools.partial(kernel, n_blk, n_rep, n_layer), out_shap...  51.1 us
    unnamed x7, local copies, waits for them, and re-layouts  3.2 us

profile of v2, /device:TPU:0, one launch (start us, length us, event | category | flops | bytes accessed | tf_op | source)
XLA Modules:
  0.0 54.3 jit_solution(2286710103830167915)
XLA Ops:
  0.0 0.0 copy-start
  0.0 1.0 %copy-done = bf16[1,1,64,4096]{3,2,1,0:T(8,128)(2,1)S(1)} copy-done((bf16[1,1,64,4096]{3,2,1,0:T(8,128)(2,1)S(1)}, bf16[1,1,64,4096]{3,2,1,0:T(8,128)(2,1)}, u32[]{:S(2)}) %copy-start) | copy-done | bytes 524312
  1.0 0.0 copy-start.1
  1.0 0.7 %copy-done.1 = bf16[1,8,128]{2,1,0:T(8,128)(2,1)S(1)} copy-done((bf16[1,8,128]{2,1,0:T(8,128)(2,1)S(1)}, bf16[1,8,128]{2,1,0:T(8,128)(2,1)}, u32[]{:S(2)}) %copy-start.1) | copy-done | bytes 2072
  1.7 0.0 copy-start.2
  1.7 0.7 %copy-done.2 = f32[1,512]{1,0:T(1,128)S(1)} copy-done((f32[1,512]{1,0:T(1,128)S(1)}, f32[1,512]{1,0:T(1,128)}, u32[]{:S(2)}) %copy-start.2) | copy-done | bytes 2072
  2.4 51.1 %influence.1 = f32[128,1024]{1,0:T(8,128)S(1)} custom-call(bf16[1,1024,4096]{2,1,0:T(8,128)(2,1)} %train_hbm.1, bf16[1,1,64,4096]{3,2,1,0:T(8,128)(2,1)S(1)} %copy-done, bf16[1,8,128]{2,1,0:T(8,128)(2,1)S(1)} %copy-done.1, f32[1,512]{1,0:T(1,128)S(1)} %copy-done.2), custom_call_target="tpu_custom_call" | custom-call | tf_op jit(solution)/shard_map/influence/pallas_call | solution.py:305
  53.5 0.8 %copy.6 = f32[1,128,1024]{2,1,0:T(8,128)} copy(f32[1,128,1024]{2,1,0:T(8,128)S(1)} %bitcast.1) | data formatting | bytes 1048576
Async XLA Ops:
  0.0 1.0 %copy-start = (bf16[1,1,64,4096]{3,2,1,0:T(8,128)(2,1)S(1)}, bf16[1,1,64,4096]{3,2,1,0:T(8,128)(2,1)}, u32[]{:S(2)}) copy-start(bf16[1,1,64,4096]{3,2,1,0:T(8,128)(2,1)} %query_hbm.1) | copy-start | bytes 1572868
  1.0 0.7 %copy-start.1 = (bf16[1,8,128]{2,1,0:T(8,128)(2,1)S(1)}, bf16[1,8,128]{2,1,0:T(8,128)(2,1)}, u32[]{:S(2)}) copy-start(bf16[1,8,128]{2,1,0:T(8,128)(2,1)} %bases_ref.1) | copy-start | bytes 6148
  1.7 0.7 %copy-start.2 = (f32[1,512]{1,0:T(1,128)S(1)}, f32[1,512]{1,0:T(1,128)}, u32[]{:S(2)}) copy-start(f32[1,512]{1,0:T(1,128)} %eigen_ref.1) | copy-start | bytes 6148

commit v3 on v2

v3 whole, which is shorter than its diff:
```python
import functools
import jax
import jax.numpy as jnp
from jax import lax
from jax.experimental import pallas as pl
from jax.experimental.pallas import tpu as pltpu
from jax.sharding import PartitionSpec as P

MESH = pl.DeviceIdType.MESH
F32 = jnp.float32
BF16 = jnp.bfloat16
LANES = 128
CHUNKS = 4
TILE = 256


def mm(a, b):
    return jnp.dot(a, b, preferred_element_type=F32)


def mm_t(a, b):
    return lax.dot_general(a, b, (((1,), (1,)), ((), ())), preferred_element_type=F32)


def one_hot(cond):
    return jnp.where(cond, 1.0, 0.0).astype(BF16)


def iota(shape, dim):
    return lax.broadcasted_iota(jnp.int32, shape, dim)


def kernel(
    n_blk, n_rep, n_layer,
    train_hbm, query_hbm, bases_hbm, eigen_hbm, out_ref,
    bases_ref, eigen_ref, train, query, raw, packet, packets, basis, eigen, square, gathered,
    total, sent, got,
    train_sem, query_sem, bases_sem, eigen_sem, pack_send, pack_recv, raw_send, raw_recv,
    up_send, up_recv, down_send, down_recv, ex_send, ex_recv,
):
    z = lax.axis_index("blk")
    rep = lax.axis_index("rep")
    layer = lax.axis_index("layer")
    n_peer = n_blk * n_rep
    me = z * n_rep + rep
    basis_rows = bases_ref.shape[0]
    eigen_rows = eigen_ref.shape[1] // LANES
    rows, flat = query.shape
    k = basis.shape[0]
    cols = flat // CHUNKS
    seqs = train.shape[1]
    share = n_blk // n_layer
    pairs = flat // LANES
    width = 2 * LANES

    bases_copy = pltpu.make_async_copy(bases_hbm.at[0], bases_ref, bases_sem)
    bases_copy.start()
    eigen_copy = pltpu.make_async_copy(eigen_hbm, eigen_ref, eigen_sem)
    eigen_copy.start()
    query_copy = pltpu.make_async_copy(query_hbm.at[0, 0], query, query_sem)
    query_copy.start()
    train_copies = [
        pltpu.make_async_copy(
            train_hbm.at[0, :, pl.ds(c * cols, cols)], train.at[c], train_sem.at[c]
        )
        for c in range(CHUNKS)
    ]

    barrier = pltpu.get_barrier_semaphore()
    peers = []
    for d in range(1, n_peer):
        peer = lax.rem(me + d, n_peer)
        peers.append({"blk": peer // n_rep, "rep": lax.rem(peer, n_rep)})
    for peer in peers:
        pl.semaphore_signal(barrier, inc=1, device_id=peer, device_id_type=MESH)
    for d in range(1, n_layer):
        pl.semaphore_signal(
            barrier, inc=1, device_id={"layer": lax.rem(layer + d, n_layer)}, device_id_type=MESH
        )

    packet[...] = jnp.zeros_like(packet)
    bases_copy.wait()
    eigen_copy.wait()
    packet[0:basis_rows, :] = bases_ref[...].astype(F32)
    for j in range(eigen_rows):
        packet[basis_rows + j:basis_rows + j + 1, :] = eigen_ref[:, j * LANES:(j + 1) * LANES]
    pl.semaphore_wait(barrier, n_peer - 1 + n_layer - 1)

    pack_copies = []
    for d in range(1, n_peer):
        copy = pltpu.make_async_remote_copy(
            src_ref=packet, dst_ref=packets.at[me],
            send_sem=pack_send.at[d], recv_sem=pack_recv.at[d],
            device_id=peers[d - 1], device_id_type=MESH,
        )
        copy.start()
        pack_copies.append(copy)
    packets[me] = packet[...]

    def raw_copy(side, to):
        return pltpu.make_async_remote_copy(
            src_ref=query_hbm.at[0, 0], dst_ref=raw,
            send_sem=raw_send.at[side], recv_sem=raw_recv,
            device_id={"blk": to}, device_id_type=MESH,
        )

    down_raw = raw_copy(0, lax.rem(z + n_blk - 1, n_blk))
    up_raw = raw_copy(1, lax.rem(z + 1, n_blk))

    @pl.when(z == 1)
    def _():
        down_raw.start()

    @pl.when(z == n_blk - 2)
    def _():
        up_raw.start()

    for copy in train_copies:
        copy.start()
    total[...] = jnp.zeros_like(total)

    wide_row, wide_col = iota((width, width), 0), iota((width, width), 1)
    row_k, col_k = iota((width, k), 0), iota((width, k), 1)
    pick_u = one_hot(col_k == 2 * (row_k & (pairs - 1)) + row_k // LANES)
    pick_v = one_hot(col_k == (row_k & (k - 1)))
    same_u = (wide_row & (LANES - 1)) // pairs == (wide_col & (LANES - 1)) // pairs
    same_v = wide_row // k == wide_col // k

    for copy in pack_copies:
        copy.wait_recv()
    for i in range(n_peer):
        basis[i * basis_rows:(i + 1) * basis_rows, :] = packets[i, 0:basis_rows, :]
        eigen[i * eigen_rows:(i + 1) * eigen_rows, :] = packets[
            i, basis_rows:basis_rows + eigen_rows, :
        ]

    u = basis[:, 0:k].astype(BF16)
    v = basis[:, k:2 * k].astype(BF16)

    def spread(pick, left, same):
        return jnp.where(same, mm_t(left, pick), 0.0).astype(BF16)

    u_turn = spread(pick_u, mm(pick_u, u).astype(BF16), same_u)
    u_back = spread(pick_u, mm_t(pick_u, u).astype(BF16), same_u)
    v_turn = spread(pick_v, mm(pick_v, v).astype(BF16), same_v)
    v_back = spread(pick_v, mm_t(pick_v, v).astype(BF16), same_v)

    eig = eigen[...]
    inverse = 1.0 / (eig + 0.1 * (jnp.sum(eig) / flat))
    group = LANES // pairs
    inverse_t = jnp.concatenate([inverse] * group, axis=0).T
    inverse_t = jnp.concatenate([inverse_t[0:k], inverse_t[k:2 * k]], axis=1)
    batch = 4
    inverse_t = jnp.concatenate([inverse_t] * batch, axis=0)

    def up_copy(s, c):
        return pltpu.make_async_remote_copy(
            src_ref=gathered.at[s, c], dst_ref=gathered.at[s, c],
            send_sem=up_send.at[s, c], recv_sem=up_recv.at[s, c],
            device_id={"blk": lax.rem(z + 1, n_blk)}, device_id_type=MESH,
        )

    def down_copy(s, c):
        return pltpu.make_async_remote_copy(
            src_ref=gathered.at[s, c], dst_ref=gathered.at[s, c],
            send_sem=down_send.at[s, c], recv_sem=down_recv.at[s, c],
            device_id={"blk": lax.rem(z + n_blk - 1, n_blk)}, device_id_type=MESH,
        )

    def turn(source, s, on_chunk):
        for c in range(flat // width):
            half = mm(source[:, c * width:(c + 1) * width], v_turn).astype(BF16).astype(F32)
            for j in range(2):
                square[pl.ds(2 * c + j, rows, stride=pairs), :] = half[:, j * LANES:(j + 1) * LANES]
        for b in range(rows // group // batch):
            stack = []
            for g in range(batch):
                at = (b * batch + g) * LANES
                t = square[at:at + LANES, :].T
                stack.append(jnp.concatenate([t[0:k], t[k:2 * k]], axis=1))
            a = jnp.concatenate(stack, axis=0).astype(BF16)
            scaled = (mm(a, u_turn) * inverse_t).astype(BF16)
            back = mm(scaled, u_back)
            for g in range(batch):
                at = (b * batch + g) * LANES
                part = back[g * k:(g + 1) * k]
                square[at:at + LANES, :] = jnp.concatenate(
                    [part[:, 0:LANES], part[:, LANES:width]], axis=0
                ).T
        per_chunk = cols // width
        for c in range(flat // width):
            x = jnp.concatenate(
                [square[pl.ds(2 * c + j, rows, stride=pairs), :] for j in range(2)], axis=1
            ).astype(BF16)
            at = (c % per_chunk) * width
            gathered[s, c // per_chunk, :, at:at + width] = mm(x, v_back).astype(BF16)
            if c % per_chunk == per_chunk - 1:
                on_chunk(c // per_chunk)

    def send_own(c):
        @pl.when(z > 1)
        def _():
            down_copy(z, c).start()

        @pl.when(z < n_blk - 2)
        def _():
            up_copy(z, c).start()

    query_copy.wait()
    turn(query, z, send_own)

    def ex_copy(s, t):
        return pltpu.make_async_remote_copy(
            src_ref=sent.at[s, t], dst_ref=got.at[layer, lax.rem(s, share), t],
            send_sem=ex_send.at[s, t], recv_sem=ex_recv.at[layer, lax.rem(s, share), t],
            device_id={"layer": s // share}, device_id_type=MESH,
        )

    def score(s, c):
        x = gathered[s, c]

        def one(t, carry):
            at = pl.ds(pl.multiple_of(t * TILE, TILE), TILE)
            total[s, :, at] += mm_t(x, train[c, at, :])

            @pl.when((c == CHUNKS - 1) & (s // share != layer))
            def _():
                sent[s, t] = total[s, :, at].astype(BF16)
                ex_copy(s, t).start()

            return carry

        lax.fori_loop(0, seqs // TILE, one, 0)

    for copy in train_copies:
        copy.wait()

    def own(c, carry):
        score(z, c)
        return carry

    lax.fori_loop(0, CHUNKS, own, 0)

    if n_blk > 1:
        @pl.when((z == 0) | (z == n_blk - 1))
        def _():
            near = 1 + (z // (n_blk - 1)) * (n_blk - 3)
            down_raw.wait_recv()
            turn(raw, near, lambda c: None)

            def close(c, carry):
                score(near, c)
                return carry

            lax.fori_loop(0, CHUNKS, close, 0)

    def step(i, carry):
        far = 1 + i // CHUNKS
        c = lax.rem(i, CHUNKS)
        above, below = z + far, z - far
        from_above = (above < n_blk) & (z + far > 1)
        from_below = (below >= 0) & (n_blk - 1 - z + far > 1)

        @pl.when(from_above)
        def _():
            down_copy(above, c).wait_recv()

            @pl.when(z > 0)
            def _():
                down_copy(above, c).start()

        @pl.when(from_below)
        def _():
            up_copy(below, c).wait_recv()

            @pl.when(z < n_blk - 1)
            def _():
                up_copy(below, c).start()

        @pl.when(from_above)
        def _():
            score(above, c)

        @pl.when(from_below)
        def _():
            score(below, c)

        return carry

    lax.fori_loop(0, (n_blk - 1) * CHUNKS, step, 0)

    tiles = seqs // TILE
    high = (2 * z) // n_blk

    def collect(i, carry):
        at, t = i // tiles, lax.rem(i, tiles)
        at = at + high * (share - 1 - 2 * at)
        span = pl.ds(pl.multiple_of(t * TILE, TILE), TILE)
        mine = layer * share + at
        for other in range(n_layer):
            @pl.when(layer != other)
            def _():
                pltpu.make_async_remote_copy(
                    src_ref=sent.at[0, 0], dst_ref=got.at[other, at, t],
                    send_sem=ex_send.at[0, 0], recv_sem=ex_recv.at[other, at, t],
                    device_id={"layer": other}, device_id_type=MESH,
                ).wait_recv()
                total[mine, :, span] += got[other, at, t].astype(F32)
        out_ref[pl.ds(pl.multiple_of(at * rows, rows), rows), span] = total[mine, :, span]
        return carry

    lax.fori_loop(0, share * tiles, collect, 0)

    for copy in pack_copies:
        copy.wait_send()

    @pl.when(z == 1)
    def _():
        down_raw.wait_send()

    @pl.when(z == n_blk - 2)
    def _():
        up_raw.wait_send()

    def drain(i, carry):
        s, c = i // CHUNKS, lax.rem(i, CHUNKS)

        @pl.when((s >= z) & (z > 0) & (s + z > 2))
        def _():
            down_copy(s, c).wait_send()

        @pl.when((s <= z) & (z < n_blk - 1) & (2 * (n_blk - 1) - s - z > 2))
        def _():
            up_copy(s, c).wait_send()

        return carry

    lax.fori_loop(0, n_blk * CHUNKS, drain, 0)

    def drain_ex(i, carry):
        s, t = i // tiles, lax.rem(i, tiles)

        @pl.when(s // share != layer)
        def _():
            ex_copy(s, t).wait_send()

        return carry

    lax.fori_loop(0, n_blk * tiles, drain_ex, 0)


def body(n_blk, n_rep, n_layer, train_grads, queries, bases, eigenvalues):
    seqs, flat = train_grads.shape[1:]
    rows = queries.shape[2]
    k = bases.shape[2] // 2
    n_peer = n_blk * n_rep
    packet_rows = -(-(bases.shape[1] + eigenvalues.shape[1] // LANES) // 8) * 8
    share = n_blk // n_layer
    cols = flat // CHUNKS
    tiles = seqs // TILE
    vmem = pl.BlockSpec(memory_space=pltpu.VMEM)
    hbm = pl.BlockSpec(memory_space=pltpu.HBM)
    dma = pltpu.SemaphoreType.DMA
    out = pl.pallas_call(
        functools.partial(kernel, n_blk, n_rep, n_layer),
        out_shape=jax.ShapeDtypeStruct((share * rows, seqs), F32),
        in_specs=[hbm] * 4,
        out_specs=vmem,
        scratch_shapes=[
            pltpu.VMEM(bases.shape[1:], BF16),
            pltpu.VMEM(eigenvalues.shape, F32),
            pltpu.VMEM((CHUNKS, seqs, cols), BF16),
            pltpu.VMEM((rows, flat), BF16),
            pltpu.VMEM((rows, flat), BF16),
            pltpu.VMEM((packet_rows, LANES), F32),
            pltpu.VMEM((n_peer, packet_rows, LANES), F32),
            pltpu.VMEM((k, 2 * k), F32),
            pltpu.VMEM((flat // LANES, LANES), F32),
            pltpu.VMEM((rows * flat // LANES, LANES), F32),
            pltpu.VMEM((n_blk, CHUNKS, rows, cols), BF16),
            pltpu.VMEM((n_blk, rows, seqs), F32),
            pltpu.VMEM((n_blk, tiles, rows, TILE), BF16),
            pltpu.VMEM((n_layer, share, tiles, rows, TILE), BF16),
            dma((CHUNKS,)),
            dma,
            dma,
            dma,
            dma((n_peer,)),
            dma((n_peer,)),
            dma((2,)),
            dma,
            dma((n_blk, CHUNKS)),
            dma((n_blk, CHUNKS)),
            dma((n_blk, CHUNKS)),
            dma((n_blk, CHUNKS)),
            dma((n_blk, tiles)),
            dma((n_layer, share, tiles)),
        ],
        compiler_params=pltpu.CompilerParams(
            collective_id=0, has_side_effects=True, vmem_limit_bytes=52 * 2**20
        ),
        name="influence",
    )(train_grads, queries, bases, eigenvalues)
    return out[None]


def solution(mesh):
    sizes = mesh.shape
    return jax.shard_map(
        functools.partial(body, sizes["blk"], sizes["rep"], sizes["layer"]),
        mesh=mesh,
        in_specs=(
            P("layer", ("groups", "blk"), None),
            P("layer", "rep", ("groups", "blk"), None),
            P("layer", ("blk", "rep"), None),
            P("layer", ("blk", "rep")),
        ),
        out_specs=P("rep", "layer", ("groups", "blk")),
        check_vma=False,
    )
```

time: 54.5 us -> 49.6 us (0.910)
  Pallas kernels: 51.1 us -> 46 us
    pallas_call x1, Pallas kernels: 51.1 us -> 46 us  [body(): pl.pallas_call(functools.partial(kernel, n_blk, n_rep, n_layer), out_shap...]
where the time goes in v3:
time: 49.6 us; the launch traced here: 49.2 us
  Pallas kernels  46 us (93%)
  local copies, waits for them, and re-layouts  3.2 us (6%)
    pallas_call x1, Pallas kernels, body(): pl.pallas_call(functools.partial(kernel, n_blk, n_rep, n_layer), out_shap...  46 us
    unnamed x7, local copies, waits for them, and re-layouts  3.2 us

profile of v3, /device:TPU:0, one launch (start us, length us, event | category | flops | bytes accessed | tf_op | source)
XLA Modules:
  0.0 49.2 jit_solution(4392588402887272483)
XLA Ops:
  0.0 0.0 copy-start
  0.0 1.0 %copy-done = bf16[1,1,64,4096]{3,2,1,0:T(8,128)(2,1)S(1)} copy-done((bf16[1,1,64,4096]{3,2,1,0:T(8,128)(2,1)S(1)}, bf16[1,1,64,4096]{3,2,1,0:T(8,128)(2,1)}, u32[]{:S(2)}) %copy-start) | copy-done | bytes 524312
  1.0 0.0 copy-start.1
  1.0 0.7 %copy-done.1 = bf16[1,8,128]{2,1,0:T(8,128)(2,1)S(1)} copy-done((bf16[1,8,128]{2,1,0:T(8,128)(2,1)S(1)}, bf16[1,8,128]{2,1,0:T(8,128)(2,1)}, u32[]{:S(2)}) %copy-start.1) | copy-done | bytes 2072
  1.7 0.0 copy-start.2
  1.7 0.7 %copy-done.2 = f32[1,512]{1,0:T(1,128)S(1)} copy-done((f32[1,512]{1,0:T(1,128)S(1)}, f32[1,512]{1,0:T(1,128)}, u32[]{:S(2)}) %copy-start.2) | copy-done | bytes 2072
  2.4 46.0 %influence.1 = f32[128,1024]{1,0:T(8,128)S(1)} custom-call(bf16[1,1024,4096]{2,1,0:T(8,128)(2,1)} %train_hbm.1, bf16[1,1,64,4096]{3,2,1,0:T(8,128)(2,1)S(1)} %copy-done, bf16[1,8,128]{2,1,0:T(8,128)(2,1)S(1)} %copy-done.1, f32[1,512]{1,0:T(1,128)S(1)} %copy-done.2), custom_call_target="tpu_custom_call" | custom-call | tf_op jit(solution)/shard_map/influence/pallas_call | solution.py:364
  48.4 0.8 %copy.6 = f32[1,128,1024]{2,1,0:T(8,128)} copy(f32[1,128,1024]{2,1,0:T(8,128)S(1)} %bitcast.1) | data formatting | bytes 1048576
Async XLA Ops:
  0.0 1.0 %copy-start = (bf16[1,1,64,4096]{3,2,1,0:T(8,128)(2,1)S(1)}, bf16[1,1,64,4096]{3,2,1,0:T(8,128)(2,1)}, u32[]{:S(2)}) copy-start(bf16[1,1,64,4096]{3,2,1,0:T(8,128)(2,1)} %query_hbm.1) | copy-start | bytes 1572868
  1.0 0.7 %copy-start.1 = (bf16[1,8,128]{2,1,0:T(8,128)(2,1)S(1)}, bf16[1,8,128]{2,1,0:T(8,128)(2,1)}, u32[]{:S(2)}) copy-start(bf16[1,8,128]{2,1,0:T(8,128)(2,1)} %bases_hbm.1) | copy-start | bytes 6148
  1.7 0.7 %copy-start.2 = (f32[1,512]{1,0:T(1,128)S(1)}, f32[1,512]{1,0:T(1,128)}, u32[]{:S(2)}) copy-start(f32[1,512]{1,0:T(1,128)} %eigen_hbm.1) | copy-start | bytes 6148

commit v4 on v3

--- a/solution.py
+++ b/solution.py
@@ -32,11 +32,11 @@
 
 def kernel(
     n_blk, n_rep, n_layer,
-    train_hbm, query_hbm, bases_hbm, eigen_hbm, out_ref,
+    train_hbm, query_hbm, bases_hbm, eigen_hbm, out_hbm,
     bases_ref, eigen_ref, train, query, raw, packet, packets, basis, eigen, square, gathered,
     total, sent, got,
     train_sem, query_sem, bases_sem, eigen_sem, pack_send, pack_recv, raw_send, raw_recv,
-    up_send, up_recv, down_send, down_recv, ex_send, ex_recv,
+    up_send, up_recv, down_send, down_recv, ex_send, ex_recv, out_sem,
 ):
     z = lax.axis_index("blk")
     rep = lax.axis_index("rep")
@@ -216,17 +216,22 @@
             device_id={"layer": s // share}, device_id_type=MESH,
         )
 
-    def score(s, c):
-        x = gathered[s, c]
+    def score(shards, c):
+        x = jnp.concatenate([gathered[s, c] for s in shards], axis=0)
 
         def one(t, carry):
             at = pl.ds(pl.multiple_of(t * TILE, TILE), TILE)
-            total[s, :, at] += mm_t(x, train[c, at, :])
-
-            @pl.when((c == CHUNKS - 1) & (s // share != layer))
+            y = mm_t(x, train[c, at, :])
+            for j, s in enumerate(shards):
+                total[s, :, at] += y[j * rows:(j + 1) * rows]
+
+            @pl.when(c == CHUNKS - 1)
             def _():
-                sent[s, t] = total[s, :, at].astype(BF16)
-                ex_copy(s, t).start()
+                for s in shards:
+                    @pl.when(s // share != layer)
+                    def _():
+                        sent[s, t] = total[s, :, at].astype(BF16)
+                        ex_copy(s, t).start()
 
             return carry
 
@@ -235,11 +240,9 @@
     for copy in train_copies:
         copy.wait()
 
-    def own(c, carry):
-        score(z, c)
-        return carry
-
-    lax.fori_loop(0, CHUNKS, own, 0)
+    if n_blk == 1:
+        for c in range(CHUNKS):
+            score([z], c)
 
     if n_blk > 1:
         @pl.when((z == 0) | (z == n_blk - 1))
@@ -249,7 +252,7 @@
             turn(raw, near, lambda c: None)
 
             def close(c, carry):
-                score(near, c)
+                score([z, near], c)
                 return carry
 
             lax.fori_loop(0, CHUNKS, close, 0)
@@ -277,13 +280,18 @@
             def _():
                 up_copy(below, c).start()
 
-        @pl.when(from_above)
-        def _():
-            score(above, c)
-
-        @pl.when(from_below)
-        def _():
-            score(below, c)
+        if n_blk > 2:
+            @pl.when((far == 1) & from_above & from_below)
+            def _():
+                score([z, above, below], c)
+
+        @pl.when(from_above & (far > 1))
+        def _():
+            score([above], c)
+
+        @pl.when(from_below & (far > 1))
+        def _():
+            score([below], c)
 
         return carry
 
@@ -291,6 +299,14 @@
 
     tiles = seqs // TILE
     high = (2 * z) // n_blk
+
+    def out_copy(at, t):
+        span = pl.ds(pl.multiple_of(t * TILE, TILE), TILE)
+        return pltpu.make_async_copy(
+            total.at[layer * share + at, :, span],
+            out_hbm.at[pl.ds(pl.multiple_of(at * rows, rows), rows), span],
+            out_sem.at[at, t],
+        )
 
     def collect(i, carry):
         at, t = i // tiles, lax.rem(i, tiles)
@@ -306,11 +322,16 @@
                     device_id={"layer": other}, device_id_type=MESH,
                 ).wait_recv()
                 total[mine, :, span] += got[other, at, t].astype(F32)
-        out_ref[pl.ds(pl.multiple_of(at * rows, rows), rows), span] = total[mine, :, span]
+        out_copy(at, t).start()
         return carry
 
     lax.fori_loop(0, share * tiles, collect, 0)
 
+    def drain_out(i, carry):
+        out_copy(i // tiles, lax.rem(i, tiles)).wait()
+        return carry
+
+    lax.fori_loop(0, share * tiles, drain_out, 0)
     for copy in pack_copies:
         copy.wait_send()
 
@@ -358,14 +379,13 @@
     share = n_blk // n_layer
     cols = flat // CHUNKS
     tiles = seqs // TILE
-    vmem = pl.BlockSpec(memory_space=pltpu.VMEM)
     hbm = pl.BlockSpec(memory_space=pltpu.HBM)
     dma = pltpu.SemaphoreType.DMA
     out = pl.pallas_call(
         functools.partial(kernel, n_blk, n_rep, n_layer),
         out_shape=jax.ShapeDtypeStruct((share * rows, seqs), F32),
         in_specs=[hbm] * 4,
-        out_specs=vmem,
+        out_specs=hbm,
         scratch_shapes=[
             pltpu.VMEM(bases.shape[1:], BF16),
             pltpu.VMEM(eigenvalues.shape, F32),
@@ -395,9 +415,10 @@
             dma((n_blk, CHUNKS)),
             dma((n_blk, tiles)),
             dma((n_layer, share, tiles)),
+            dma((share, tiles)),
         ],
         compiler_params=pltpu.CompilerParams(
-            collective_id=0, has_side_effects=True, vmem_limit_bytes=52 * 2**20
+            collective_id=0, has_side_effects=True, vmem_limit_bytes=63 * 2**20
         ),
         name="influence",
     )(train_grads, queries, bases, eigenvalues)

time: 49.6 us -> 48.7 us (0.982)
  local copies, waits for them, and re-layouts: 3.2 us -> 1.89 us
    unnamed x7 -> x1, local copies, waits for them, and re-layouts: 3.2 us -> 1.89 us
where the time goes in v4:
time: 48.7 us; the launch traced here: 47.8 us
  Pallas kernels  46 us (94%)
  local copies, waits for them, and re-layouts  1.89 us (4%)
    pallas_call x1, Pallas kernels, body(): pl.pallas_call(functools.partial(kernel, n_blk, n_rep, n_layer), out_shap...  46 us
    unnamed x1, local copies, waits for them, and re-layouts  1.89 us

profile of v4, /device:TPU:0, one launch (start us, length us, event | category | flops | bytes accessed | tf_op | source)
XLA Modules:
  0.0 47.8 jit_solution(10988512993085802006)
XLA Ops:
  0.0 46.0 %influence.1 = f32[128,1024]{1,0:T(8,128)} custom-call(bf16[1,1024,4096]{2,1,0:T(8,128)(2,1)} %train_hbm.1, bf16[1,1,64,4096]{3,2,1,0:T(8,128)(2,1)} %query_hbm.1, bf16[1,8,128]{2,1,0:T(8,128)(2,1)} %bases_hbm.1, f32[1,512]{1,0:T(1,128)} %eigen_hbm.1), custom_call_target="tpu_custom_call" | custom-call | tf_op jit(solution)/shard_map/influence/pallas_call | solution.py:384
  46.0 1.9 %copy.6 = f32[1,128,1024]{2,1,0:T(8,128)} copy(f32[1,128,1024]{2,1,0:T(8,128)} %bitcast.1) | data formatting | bytes 1048576

commit v5 on v4

--- a/solution.py
+++ b/solution.py
@@ -10,7 +10,7 @@
 F32 = jnp.float32
 BF16 = jnp.bfloat16
 LANES = 128
-CHUNKS = 4
+CHUNKS = 8
 TILE = 256
 
 
@@ -32,11 +32,11 @@
 
 def kernel(
     n_blk, n_rep, n_layer,
-    train_hbm, query_hbm, bases_hbm, eigen_hbm, out_hbm,
+    train_hbm, query_hbm, bases_hbm, eigen_hbm, own_hbm, got_hbm,
     bases_ref, eigen_ref, train, query, raw, packet, packets, basis, eigen, square, gathered,
-    total, sent, got,
+    total, sent,
     train_sem, query_sem, bases_sem, eigen_sem, pack_send, pack_recv, raw_send, raw_recv,
-    up_send, up_recv, down_send, down_recv, ex_send, ex_recv, out_sem,
+    up_send, up_recv, down_send, down_recv, ex_send, ex_recv, own_sem,
 ):
     z = lax.axis_index("blk")
     rep = lax.axis_index("rep")
@@ -209,11 +209,25 @@
     query_copy.wait()
     turn(query, z, send_own)
 
+    def place(s, t):
+        return (
+            pl.ds(pl.multiple_of(lax.rem(s, share) * rows, rows), rows),
+            pl.ds(pl.multiple_of(t * TILE, TILE), TILE),
+        )
+
     def ex_copy(s, t):
+        slot = lax.rem(layer - s // share + n_layer - 1, n_layer)
         return pltpu.make_async_remote_copy(
-            src_ref=sent.at[s, t], dst_ref=got.at[layer, lax.rem(s, share), t],
-            send_sem=ex_send.at[s, t], recv_sem=ex_recv.at[layer, lax.rem(s, share), t],
+            src_ref=sent.at[s, t], dst_ref=got_hbm.at[(slot, *place(s, t))],
+            send_sem=ex_send.at[s, t], recv_sem=ex_recv.at[slot, lax.rem(s, share), t],
             device_id={"layer": s // share}, device_id_type=MESH,
+        )
+
+    def own_copy(s, t):
+        rows_at, cols_at = place(s, t)
+        return pltpu.make_async_copy(
+            total.at[s, :, cols_at], own_hbm.at[rows_at, cols_at],
+            own_sem.at[lax.rem(s, share), t],
         )
 
     def score(shards, c):
@@ -233,6 +247,10 @@
                         sent[s, t] = total[s, :, at].astype(BF16)
                         ex_copy(s, t).start()
 
+                    @pl.when(s // share == layer)
+                    def _():
+                        own_copy(s, t).start()
+
             return carry
 
         lax.fori_loop(0, seqs // TILE, one, 0)
@@ -297,41 +315,6 @@
 
     lax.fori_loop(0, (n_blk - 1) * CHUNKS, step, 0)
 
-    tiles = seqs // TILE
-    high = (2 * z) // n_blk
-
-    def out_copy(at, t):
-        span = pl.ds(pl.multiple_of(t * TILE, TILE), TILE)
-        return pltpu.make_async_copy(
-            total.at[layer * share + at, :, span],
-            out_hbm.at[pl.ds(pl.multiple_of(at * rows, rows), rows), span],
-            out_sem.at[at, t],
-        )
-
-    def collect(i, carry):
-        at, t = i // tiles, lax.rem(i, tiles)
-        at = at + high * (share - 1 - 2 * at)
-        span = pl.ds(pl.multiple_of(t * TILE, TILE), TILE)
-        mine = layer * share + at
-        for other in range(n_layer):
-            @pl.when(layer != other)
-            def _():
-                pltpu.make_async_remote_copy(
-                    src_ref=sent.at[0, 0], dst_ref=got.at[other, at, t],
-                    send_sem=ex_send.at[0, 0], recv_sem=ex_recv.at[other, at, t],
-                    device_id={"layer": other}, device_id_type=MESH,
-                ).wait_recv()
-                total[mine, :, span] += got[other, at, t].astype(F32)
-        out_copy(at, t).start()
-        return carry
-
-    lax.fori_loop(0, share * tiles, collect, 0)
-
-    def drain_out(i, carry):
-        out_copy(i // tiles, lax.rem(i, tiles)).wait()
-        return carry
-
-    lax.fori_loop(0, share * tiles, drain_out, 0)
     for copy in pack_copies:
         copy.wait_send()
 
@@ -365,8 +348,20 @@
         def _():
             ex_copy(s, t).wait_send()
 
+        @pl.when(s // share == layer)
+        def _():
+            own_copy(s, t).wait()
+            for slot in range(n_layer - 1):
+                pltpu.make_async_remote_copy(
+                    src_ref=sent.at[s, t], dst_ref=got_hbm.at[(slot, *place(s, t))],
+                    send_sem=ex_send.at[s, t],
+                    recv_sem=ex_recv.at[slot, lax.rem(s, share), t],
+                    device_id={"layer": lax.rem(layer + 1, n_layer)}, device_id_type=MESH,
+                ).wait_recv()
+
         return carry
 
+    tiles = seqs // TILE
     lax.fori_loop(0, n_blk * tiles, drain_ex, 0)
 
 
@@ -381,11 +376,14 @@
     tiles = seqs // TILE
     hbm = pl.BlockSpec(memory_space=pltpu.HBM)
     dma = pltpu.SemaphoreType.DMA
-    out = pl.pallas_call(
+    own, got = pl.pallas_call(
         functools.partial(kernel, n_blk, n_rep, n_layer),
-        out_shape=jax.ShapeDtypeStruct((share * rows, seqs), F32),
+        out_shape=(
+            jax.ShapeDtypeStruct((share * rows, seqs), F32),
+            jax.ShapeDtypeStruct((max(n_layer - 1, 1), share * rows, seqs), BF16),
+        ),
         in_specs=[hbm] * 4,
-        out_specs=hbm,
+        out_specs=(hbm, hbm),
         scratch_shapes=[
             pltpu.VMEM(bases.shape[1:], BF16),
             pltpu.VMEM(eigenvalues.shape, F32),
@@ -400,7 +398,6 @@
             pltpu.VMEM((n_blk, CHUNKS, rows, cols), BF16),
             pltpu.VMEM((n_blk, rows, seqs), F32),
             pltpu.VMEM((n_blk, tiles, rows, TILE), BF16),
-            pltpu.VMEM((n_layer, share, tiles, rows, TILE), BF16),
             dma((CHUNKS,)),
             dma,
             dma,
@@ -422,7 +419,9 @@
         ),
         name="influence",
     )(train_grads, queries, bases, eigenvalues)
-    return out[None]
+    for slot in range(n_layer - 1):
+        own = own + got[slot].astype(F32)
+    return own[None]
 
 
 def solution(mesh):

time: 48.7 us -> 50.2 us (1.031); the launches traced: 47.8 us -> 50 us
  Pallas kernels: 46 us -> 48 us
  other arithmetic: 0 us -> 1.96 us
  local copies, waits for them, and re-layouts: 1.89 us -> 0 us
    pallas_call x1, Pallas kernels: 46 us -> 48 us  [body(): pl.pallas_call(functools.partial(kernel, n_blk, n_rep, n_layer), out_shap...]
    broadcast_in_dim x0 -> x1, other arithmetic: none -> 1.96 us  [body(): return own[None]]
    unnamed x1 -> x0, local copies, waits for them, and re-layouts: 1.89 us -> none
where the time goes in v5:
time: 50.2 us; the launch traced here: 50 us
  Pallas kernels  48 us (96%)
  other arithmetic  1.96 us (4%)
    pallas_call x1, Pallas kernels, body(): pl.pallas_call(functools.partial(kernel, n_blk, n_rep, n_layer), out_shap...  48 us
    broadcast_in_dim x1, other arithmetic, body(): return own[None]  1.96 us

profile of v5, /device:TPU:0, one launch (start us, length us, event | category | flops | bytes accessed | tf_op | source)
XLA Modules:
  0.0 50.0 jit_solution(12044166859307507525)
XLA Ops:
  0.0 48.0 %influence.1 = (f32[128,1024]{1,0:T(8,128)}, bf16[1,128,1024]{2,1,0:T(8,128)(2,1)}) custom-call(bf16[1,1024,4096]{2,1,0:T(8,128)(2,1)} %train_hbm.1, bf16[1,1,64,4096]{3,2,1,0:T(8,128)(2,1)} %query_hbm.1, bf16[1,8,128]{2,1,0:T(8,128)(2,1)} %bases_hbm.1, f32[1,512]{1,0:T(1,128)} %eigen_hbm.1), custom_call_target="tpu_custom_call" | custom-call | tf_op jit(solution)/shard_map/influence/pallas_call | solution.py:379
  48.1 2.0 %fusion = f32[1,128,1024]{2,1,0:T(8,128)} fusion(f32[128,1024]{1,0:T(8,128)} %get-tuple-element.7, bf16[1,128,1024]{2,1,0:T(8,128)(2,1)} %get-tuple-element.8), kind=kLoop, calls=%fused_computation.1 | loop fusion | flops 262144 | bytes 1310720 | tf_op jit(solution)/shard_map/broadcast_in_dim | solution.py:424

commit v6 on v4

--- a/solution.py
+++ b/solution.py
@@ -217,11 +217,11 @@
         )
 
     def score(shards, c):
-        x = jnp.concatenate([gathered[s, c] for s in shards], axis=0)
+        x = jnp.concatenate([gathered[s, c] for s in shards], axis=0).T
 
         def one(t, carry):
             at = pl.ds(pl.multiple_of(t * TILE, TILE), TILE)
-            y = mm_t(x, train[c, at, :])
+            y = mm(train[c, at, :], x).T
             for j, s in enumerate(shards):
                 total[s, :, at] += y[j * rows:(j + 1) * rows]
 
@@ -296,6 +296,32 @@
         return carry
 
     lax.fori_loop(0, (n_blk - 1) * CHUNKS, step, 0)
+
+    for copy in pack_copies:
+        copy.wait_send()
+
+    @pl.when(z == 1)
+    def _():
+        down_raw.wait_send()
+
+    @pl.when(z == n_blk - 2)
+    def _():
+        up_raw.wait_send()
+
+    def drain(i, carry):
+        s, c = i // CHUNKS, lax.rem(i, CHUNKS)
+
+        @pl.when((s >= z) & (z > 0) & (s + z > 2))
+        def _():
+            down_copy(s, c).wait_send()
+
+        @pl.when((s <= z) & (z < n_blk - 1) & (2 * (n_blk - 1) - s - z > 2))
+        def _():
+            up_copy(s, c).wait_send()
+
+        return carry
+
+    lax.fori_loop(0, n_blk * CHUNKS, drain, 0)
 
     tiles = seqs // TILE
     high = (2 * z) // n_blk
@@ -332,32 +358,6 @@
         return carry
 
     lax.fori_loop(0, share * tiles, drain_out, 0)
-    for copy in pack_copies:
-        copy.wait_send()
-
-    @pl.when(z == 1)
-    def _():
-        down_raw.wait_send()
-
-    @pl.when(z == n_blk - 2)
-    def _():
-        up_raw.wait_send()
-
-    def drain(i, carry):
-        s, c = i // CHUNKS, lax.rem(i, CHUNKS)
-
-        @pl.when((s >= z) & (z > 0) & (s + z > 2))
-        def _():
-            down_copy(s, c).wait_send()
-
-        @pl.when((s <= z) & (z < n_blk - 1) & (2 * (n_blk - 1) - s - z > 2))
-        def _():
-            up_copy(s, c).wait_send()
-
-        return carry
-
-    lax.fori_loop(0, n_blk * CHUNKS, drain, 0)
-
     def drain_ex(i, carry):
         s, t = i // tiles, lax.rem(i, tiles)
 

time: 48.7 us -> 48.2 us (0.990); the launches traced: 47.8 us -> 47.9 us
  no operation moved by 1% of the time
where the time goes in v6:
time: 48.2 us; the launch traced here: 47.9 us
  Pallas kernels  46 us (95%)
  local copies, waits for them, and re-layouts  1.89 us (4%)
    pallas_call x1, Pallas kernels, body(): pl.pallas_call(functools.partial(kernel, n_blk, n_rep, n_layer), out_shap...  46 us
    unnamed x1, local copies, waits for them, and re-layouts  1.89 us

profile of v6, /device:TPU:0, one launch (start us, length us, event | category | flops | bytes accessed | tf_op | source)
XLA Modules:
  0.0 47.9 jit_solution(7839177626435217609)
XLA Ops:
  0.0 46.0 %influence.1 = f32[128,1024]{1,0:T(8,128)} custom-call(bf16[1,1024,4096]{2,1,0:T(8,128)(2,1)} %train_hbm.1, bf16[1,1,64,4096]{3,2,1,0:T(8,128)(2,1)} %query_hbm.1, bf16[1,8,128]{2,1,0:T(8,128)(2,1)} %bases_hbm.1, f32[1,512]{1,0:T(1,128)} %eigen_hbm.1), custom_call_target="tpu_custom_call" | custom-call | tf_op jit(solution)/shard_map/influence/pallas_call | solution.py:384
  46.0 1.9 %copy.6 = f32[1,128,1024]{2,1,0:T(8,128)} copy(f32[1,128,1024]{2,1,0:T(8,128)} %bitcast.1) | data formatting | bytes 1048576
